TPU v7x, 512 devices: a whole 4x4x16 slice. The times are simulated.
512 devices in a mesh: ka: 64 (over z, x_hi, core), ga: 8 (over y, x_lo).
Axes of the slice: x: 4 (x_hi: 2, x_lo: 2; x = x_hi * 2 + x_lo), y: 4, z: 16, core: 2. Of those that a mesh axis runs over, the one named last changes fastest.
Arguments:
- orbitals: bfloat16 [128, 4096, 256], P('ka', 'ga'), may hold values from -1.5 to 1.5
- minus_table: int32 [2, 128], replicated, may hold values from 0 to 127, as said below
- points: int32 [512], replicated, may hold values from 0 to 4095, as said below
Outputs:
- pair_matrix: float32 [512, 2, 2, 4096], P('ka', None, None, 'ga')
Inputs may be any that keep to these rules, and one draw needn't show every extreme that they name: `minus_table`: row q holds (k - s) mod 128 for every k, with one shift s for the row that is a nonzero multiple of 2; the two rows have different shifts. `points`: distinct grid indices; 0 and 4095 are among them.
All inputs are finite; a program needn't handle non-finite values.
Results may differ from a plain program's by a relative error of at most 0.0012.
Values may be sent and summed in bfloat16 or wider, within the bound.
A program may use at most 64 MiB of HBM per device.

v0:
```python
import math

import jax
import jax.numpy as jnp
from jax import lax
from jax.sharding import PartitionSpec as P


def from_behind(block, axis, distance):
    devices = range(lax.axis_size(axis))
    route = [((i - distance) % len(devices), i) for i in devices]
    return lax.ppermute(block, axis, route)


def pair_block(field_rows, collected):
    halfway = collected.shape[-1] // 2
    rotated = jnp.concatenate([-collected[:, :, halfway:], collected[:, :, :halfway]], axis=2)
    stacked = jnp.concatenate([collected, rotated], axis=1)
    product = jnp.einsum("kpc,kgc->kpg", stacked, field_rows, preferred_element_type=jnp.float32)
    rounded = lax.optimization_barrier(product.astype(jnp.bfloat16))
    return rounded.astype(jnp.float32)


def hadamard(own_field, other_field, length):
    real_part = jnp.sum(
        own_field[:, :length] * other_field[:, :length]
        + own_field[:, length:] * other_field[:, length:],
        axis=0,
    )
    imag_part = jnp.sum(
        own_field[:, length:] * other_field[:, :length]
        - own_field[:, :length] * other_field[:, length:],
        axis=0,
    )
    return jnp.stack([real_part, imag_part], axis=1)


def on_device(orbitals, minus_table, points):
    kdevice, slab_size, channels = orbitals.shape
    cycle_size = lax.axis_size("ka")
    total_k = kdevice * cycle_size
    transfers = minus_table.shape[0]
    first_kpoint = lax.axis_index("ka") * kdevice
    local_rows = points - lax.axis_index("ga") * slab_size
    inside = (local_rows >= 0) & (local_rows < slab_size)
    clipped = jnp.clip(local_rows, 0, slab_size - 1)

    def collect(fields):
        picked = jnp.take(fields, clipped, axis=-2).astype(jnp.float32)
        return jnp.where(inside[:, None], picked, 0.0)

    own_rows = lax.psum(collect(orbitals).astype(jnp.bfloat16), "ga")
    targets = lax.dynamic_slice_in_dim(minus_table, first_kpoint, 1, 1)[:, 0]
    offsets = (first_kpoint - targets) % total_k // kdevice
    sections = (cycle_size - 1).bit_length()
    series = []
    for transfer in range(transfers):
        current = orbitals
        for section in range(sections):
            arrived = from_behind(current, "ka", 1 << section)
            current = jnp.where(offsets[transfer] >> section & 1 == 1, arrived, current)
        series.append(current)
    moving = jnp.stack(series)
    shifted_rows = lax.psum(collect(moving).astype(jnp.bfloat16), "ga")
    factor = 1.0 / math.sqrt(total_k)
    length = lax.axis_size("ka") * (points.shape[0] // cycle_size)
    own_field = pair_block(orbitals, own_rows)
    pieces = []
    for transfer in range(transfers):
        other_field = pair_block(moving[transfer], shifted_rows[transfer])
        pieces.append(hadamard(own_field, other_field, length))
    summed = lax.psum_scatter(jnp.stack(pieces, axis=1), "ka", scatter_dimension=0, tiled=True)
    return summed * factor


def solution(mesh):
    placed = (P("ka", "ga", None), P(), P())
    return jax.shard_map(
        on_device, mesh=mesh, in_specs=placed, out_specs=P("ka", None, None, "ga"), check_vma=False
    )
```

profile of v0, /device:TPU:1, one launch (start us, length us, event | category | flops | bytes accessed | tf_op | source)
XLA Modules:
  0.0 1014.0 jit_solution(2717944493997630326)
XLA Ops:
  8.1 6.0 collective-permute-start
  16.9 3.4 collective-permute-done
  22.4 3.5 collective-permute-start.1
  25.9 4.7 collective-permute-start.6
  31.8 7.5 collective-permute-done.1
  41.4 8.2 collective-permute-done.6
  49.7 3.0 collective-permute-start.7
  55.9 2.9 collective-permute-start.3
  58.9 11.7 %collective-permute-done.7 = bf16[2,512,256]{2,0,1:T(2,128)(2,1)S(1)} collective-permute-done((bf16[2,512,256]{2,0,1:T(2,128)(2,1)S(1)}, bf16[2,512,256]{2,0,1:T(2,128)(2,1)S(1)}, u32[]{:S(2)}, u32[]{:S(2)}) %collective-permute-start.7) | collective-permute-done | bytes 524320 | tf_op jit(solution)/shard_map/ppermute | solution.py:12
  73.8 11.4 %collective-permute-done.3 = bf16[2,512,256]{2,0,1:T(2,128)(2,1)S(1)} collective-permute-done((bf16[2,512,256]{2,0,1:T(2,128)(2,1)S(1)}, bf16[2,512,256]{2,0,1:T(2,128)(2,1)S(1)}, u32[]{:S(2)}, u32[]{:S(2)}) %collective-permute-start.3) | collective-permute-done | bytes 524320 | tf_op jit(solution)/shard_map/ppermute | solution.py:12
  85.3 2.4 collective-permute-start.4
  87.6 9.8 collective-permute-done.8
  97.5 13.3 %collective-permute-start.9 = (bf16[2,512,256]{2,0,1:T(2,128)(2,1)S(1)}, bf16[2,512,256]{2,0,1:T(2,128)(2,1)S(1)}, u32[]{:S(2)}, u32[]{:S(2)}) collective-permute-start(bf16[2,512,256]{2,0,1:T(2,128)(2,1)S(1)} %bitcast.59), channel_id=1, source_target_pairs={{384,0},{392,8},{400,16},{408,24},{416,32},{424,40},{432,48},{440,... | collective-permute-start | bytes 1572872 | tf_op jit(solution)/shard_map/ppermute | solution.py:12
  112.1 9.0 collective-permute-start.5
  121.2 24.3 %collective-permute-done.9 = bf16[2,512,256]{2,0,1:T(2,128)(2,1)S(1)} collective-permute-done((bf16[2,512,256]{2,0,1:T(2,128)(2,1)S(1)}, bf16[2,512,256]{2,0,1:T(2,128)(2,1)S(1)}, u32[]{:S(2)}, u32[]{:S(2)}) %collective-permute-start.9) | collective-permute-done | bytes 524320 | tf_op jit(solution)/shard_map/ppermute | solution.py:12
  145.5 4.1 collective-permute-start.10
  150.8 3.0 gather_fusion
  154.8 25.3 %collective-permute-done.5 = bf16[2,512,256]{2,0,1:T(2,128)(2,1)} collective-permute-done((bf16[2,512,256]{2,0,1:T(2,128)(2,1)S(1)}, bf16[2,512,256]{2,0,1:T(2,128)(2,1)}, u32[]{:S(2)}, u32[]{:S(2)}) %collective-permute-start.5) | collective-permute-done | bytes 524320 | tf_op jit(solution)/shard_map/ppermute | solution.py:12
  181.3 99.0 %collective-permute-done.10 = bf16[2,512,256]{2,0,1:T(2,128)(2,1)S(1)} collective-permute-done((bf16[2,512,256]{2,0,1:T(2,128)(2,1)S(1)}, bf16[2,512,256]{2,0,1:T(2,128)(2,1)S(1)}, u32[]{:S(2)}, u32[]{:S(2)}) %collective-permute-start.10) | collective-permute-done | bytes 524320 | tf_op jit(solution)/shard_map/ppermute | solution.py:12
  282.6 3.8 gather_fusion.1
  288.0 157.1 %all-reduce.7.cloned.1.call-done = (bf16[2,2,512,256]{3,2,1,0:T(8,128)(2,1)}, bf16[2,512,256]{2,1,0:T(8,128)(2,1)}) async-done(((bf16[2,2,512,256]{3,2,1,0:T(8,128)(2,1)}, bf16[2,512,256]{2,1,0:T(8,128)(2,1)}), (bf16[2,2,512,256]{3,2,1,0:T(8,128)(2,1)}, bf16[2,512,256]{2,1,0:T(8,128)(2,1)})) %all-reduce.7.cloned.1.call-update) | async-done | bytes 1572880 | tf_op jit(solution)/shard_map/psum | solution.py:64
  451.1 2.4 add_reduce_fusion.1
  460.2 3.8 pad_maximum_fusion
  466.0 539.7 %all-reduce.5.cloned.1.call-done = f32[512,2,2,512]{3,2,1,0:T(2,128)} async-done(((f32[512,2,2,512]{3,2,1,0:T(2,128)}), f32[512,2,2,512]{3,2,1,0:T(2,128)}) %all-reduce.5.cloned.1.call-update) | async-done | bytes 4194320
  (55 shorter events, 33.1 us)
Async XLA Ops:
  6.5 438.5 %all-reduce.7.cloned.1.call-start = ((), (), s32[]{:S(2)}) async-start(), calls=%async_computation.1 | async-start | bytes 3145728 | tf_op jit(solution)/shard_map/psum | solution.py:64
  8.1 12.2 %collective-permute-start = (bf16[2,512,256]{2,0,1:T(2,128)(2,1)S(1)}, bf16[2,512,256]{2,0,1:T(2,128)(2,1)S(1)}, u32[]{:S(2)}, u32[]{:S(2)}) collective-permute-start(bf16[2,512,256]{2,0,1:T(2,128)(2,1)S(1)} %copy.10), channel_id=1, source_target_pairs={{504,0},{0,8},{8,16},{16,24},{24,32},{32,40},{40,48},{48,56},{56,6... | collective-permute-start | bytes 1572872 | tf_op jit(solution)/shard_map/ppermute | solution.py:12
  22.4 16.9 %collective-permute-start.1 = (bf16[2,512,256]{2,0,1:T(2,128)(2,1)S(1)}, bf16[2,512,256]{2,0,1:T(2,128)(2,1)S(1)}, u32[]{:S(2)}, u32[]{:S(2)}) collective-permute-start(bf16[2,512,256]{2,0,1:T(2,128)(2,1)S(1)} %get-tuple-element.17), channel_id=1, source_target_pairs={{496,0},{504,8},{0,16},{8,24},{16,32},{24,40},{32,48},{40,56},{48,... | collective-permute-start | bytes 1572872 | tf_op jit(solution)/shard_map/ppermute | solution.py:12
  25.9 23.8 %collective-permute-start.6 = (bf16[2,512,256]{2,0,1:T(2,128)(2,1)S(1)}, bf16[2,512,256]{2,0,1:T(2,128)(2,1)S(1)}, u32[]{:S(2)}, u32[]{:S(2)}) collective-permute-start(bf16[2,512,256]{2,0,1:T(2,128)(2,1)S(1)} %get-tuple-element.18), channel_id=1, source_target_pairs={{496,0},{504,8},{0,16},{8,24},{16,32},{24,40},{32,48},{40,56},{48,... | collective-permute-start | bytes 1572872 | tf_op jit(solution)/shard_map/ppermute | solution.py:12
  39.3 16.6 %collective-permute-start.2 = (bf16[2,512,256]{2,0,1:T(2,128)(2,1)S(1)}, bf16[2,512,256]{2,0,1:T(2,128)(2,1)S(1)}, u32[]{:S(2)}, u32[]{:S(2)}) collective-permute-start(bf16[2,512,256]{2,0,1:T(2,128)(2,1)S(1)} %bitcast.62), channel_id=1, source_target_pairs={{480,0},{488,8},{496,16},{504,24},{0,32},{8,40},{16,48},{24,56},{3... | collective-permute-start | bytes 1572872 | tf_op jit(solution)/shard_map/ppermute | solution.py:12
  49.7 20.9 %collective-permute-start.7 = (bf16[2,512,256]{2,0,1:T(2,128)(2,1)S(1)}, bf16[2,512,256]{2,0,1:T(2,128)(2,1)S(1)}, u32[]{:S(2)}, u32[]{:S(2)}) collective-permute-start(bf16[2,512,256]{2,0,1:T(2,128)(2,1)S(1)} %bitcast.63), channel_id=1, source_target_pairs={{480,0},{488,8},{496,16},{504,24},{0,32},{8,40},{16,48},{24,56},{3... | collective-permute-start | bytes 1572872 | tf_op jit(solution)/shard_map/ppermute | solution.py:12
  55.9 29.3 %collective-permute-start.3 = (bf16[2,512,256]{2,0,1:T(2,128)(2,1)S(1)}, bf16[2,512,256]{2,0,1:T(2,128)(2,1)S(1)}, u32[]{:S(2)}, u32[]{:S(2)}) collective-permute-start(bf16[2,512,256]{2,0,1:T(2,128)(2,1)S(1)} %bitcast.64), channel_id=1, source_target_pairs={{448,0},{456,8},{464,16},{472,24},{480,32},{488,40},{496,48},{504,... | collective-permute-start | bytes 1572872 | tf_op jit(solution)/shard_map/ppermute | solution.py:12
  70.6 41.5 %copy-start.4 = (s32[512]{0:T(512)S(1)}, s32[512]{0:T(512)}, u32[]{:S(2)}) copy-start(s32[512]{0:T(512)} %param.5) | copy-start | bytes 6148
  70.6 26.8 %collective-permute-start.8 = (bf16[2,512,256]{2,0,1:T(2,128)(2,1)S(1)}, bf16[2,512,256]{2,0,1:T(2,128)(2,1)S(1)}, u32[]{:S(2)}, u32[]{:S(2)}) collective-permute-start(bf16[2,512,256]{2,0,1:T(2,128)(2,1)S(1)} %bitcast.65), channel_id=1, source_target_pairs={{448,0},{456,8},{464,16},{472,24},{480,32},{488,40},{496,48},{504,... | collective-permute-start | bytes 1572872 | tf_op jit(solution)/shard_map/ppermute | solution.py:12
  85.3 26.8 %collective-permute-start.4 = (bf16[2,512,256]{2,0,1:T(2,128)(2,1)S(1)}, bf16[2,512,256]{2,0,1:T(2,128)(2,1)S(1)}, u32[]{:S(2)}, u32[]{:S(2)}) collective-permute-start(bf16[2,512,256]{2,0,1:T(2,128)(2,1)S(1)} %bitcast.58), channel_id=1, source_target_pairs={{384,0},{392,8},{400,16},{408,24},{416,32},{424,40},{432,48},{440,... | collective-permute-start | bytes 1572872 | tf_op jit(solution)/shard_map/ppermute | solution.py:12
  97.5 53.4 %copy-start = (bf16[2,512,256]{2,1,0:T(8,128)(2,1)S(1)}, bf16[2,512,256]{2,1,0:T(8,128)(2,1)}, u32[]{:S(2)}) copy-start(bf16[2,512,256]{2,1,0:T(8,128)(2,1)} %param.3) | copy-start | bytes 1572868
  97.5 47.9 %collective-permute-start.9 = (bf16[2,512,256]{2,0,1:T(2,128)(2,1)S(1)}, bf16[2,512,256]{2,0,1:T(2,128)(2,1)S(1)}, u32[]{:S(2)}, u32[]{:S(2)}) collective-permute-start(bf16[2,512,256]{2,0,1:T(2,128)(2,1)S(1)} %bitcast.59), channel_id=1, source_target_pairs={{384,0},{392,8},{400,16},{408,24},{416,32},{424,40},{432,48},{440,... | collective-permute-start | bytes 1572872 | tf_op jit(solution)/shard_map/ppermute | solution.py:12
  112.1 68.0 %collective-permute-start.5 = (bf16[2,512,256]{2,0,1:T(2,128)(2,1)S(1)}, bf16[2,512,256]{2,0,1:T(2,128)(2,1)}, u32[]{:S(2)}, u32[]{:S(2)}) collective-permute-start(bf16[2,512,256]{2,0,1:T(2,128)(2,1)S(1)} %bitcast.60), channel_id=1, source_target_pairs={{256,0},{264,8},{272,16},{280,24},{288,32},{296,40},{304,48},{312,... | collective-permute-start | bytes 1572872 | tf_op jit(solution)/shard_map/ppermute | solution.py:12
  145.5 134.7 %collective-permute-start.10 = (bf16[2,512,256]{2,0,1:T(2,128)(2,1)S(1)}, bf16[2,512,256]{2,0,1:T(2,128)(2,1)S(1)}, u32[]{:S(2)}, u32[]{:S(2)}) collective-permute-start(bf16[2,512,256]{2,0,1:T(2,128)(2,1)S(1)} %bitcast.61), channel_id=1, source_target_pairs={{256,0},{264,8},{272,16},{280,24},{288,32},{296,40},{304,48},{312,... | collective-permute-start | bytes 1572872 | tf_op jit(solution)/shard_map/ppermute | solution.py:12
  280.3 0.8 copy-start.1
  287.7 717.9 %all-reduce.5.cloned.1.call-start = ((), (), s32[]{:S(2)}) async-start(), calls=%async_computation | async-start | bytes 8388608
  445.0 1.5 copy-start.2
  447.3 1.0 copy-start.3
Sparse Core Ops, SparseCore 0:
  287.8 157.1 all-reduce.6
  464.1 541.4 all-reduce.4
where the time goes:
time: 1010 us
  waiting for transfers between devices  899 us (89%)
  starting transfers between devices  53.1 us (5%)
  other arithmetic  21.9 us (2%)
  between operations  21.8 us (2%)
  local copies, waits for them, and re-layouts  15.6 us (2%)
    unnamed x3, waiting for transfers between devices  540 us
    ppermute x11, waiting for transfers between devices, from_behind(): return lax.ppermute(block, axis, route)  203 us
    psum x1, waiting for transfers between devices, on_device(): shifted_rows = lax.psum(collect(moving).astype(jnp.bfloat16), 'ga')  157 us
    ppermute x11, starting transfers between devices, from_behind(): return lax.ppermute(block, axis, route)  52.9 us
  transfers between devices with their start and end apart: 13, of which 12 were waited for; matrix products, arithmetic and copies ran while one was open for 1% of the time, Pallas kernels for 0%

commit v1 on v0

v1 whole, which is shorter than its diff:
```python
import math

import jax
import jax.numpy as jnp
from jax import lax
from jax.sharding import PartitionSpec as P


def on_device(orbitals, minus_table, points):
    kdevice, slab_size, channels = orbitals.shape
    cycle_size = lax.axis_size("ka")
    total_k = kdevice * cycle_size
    transfers = minus_table.shape[0]
    npts = points.shape[0]
    block = npts // cycle_size
    half = channels // 2
    local_rows = points - lax.axis_index("ga") * slab_size
    hot = (local_rows[:, None] == jnp.arange(slab_size)[None, :]).astype(jnp.bfloat16)
    picked = jnp.einsum("pg,kgc->kpc", hot, orbitals, preferred_element_type=jnp.float32)
    rows = lax.psum(picked.astype(jnp.bfloat16), "ga")
    rotated = jnp.concatenate([-rows[:, :, half:], rows[:, :, :half]], axis=2)
    parts = jnp.stack(
        [r.reshape(kdevice, cycle_size, block, channels) for r in (rows, rotated)], axis=2
    )
    stacked = parts.reshape(kdevice, cycle_size * 2 * block, channels)
    product = jnp.einsum("kpc,kgc->kpg", stacked, orbitals, preferred_element_type=jnp.float32)
    field = product.astype(jnp.bfloat16).reshape(kdevice, cycle_size, 2 * block, slab_size)
    arrived = lax.all_to_all(field.transpose(1, 0, 2, 3), "ka", 0, 0, tiled=True)
    own = arrived.reshape(total_k, 2, block, slab_size)
    twice = jnp.concatenate([own, own], axis=0)
    mine = own.astype(jnp.float32)
    pieces = []
    for transfer in range(transfers):
        other = lax.dynamic_slice_in_dim(twice, minus_table[transfer, 0], total_k, 0).astype(jnp.float32)
        real = jnp.sum(mine[:, 0] * other[:, 0] + mine[:, 1] * other[:, 1], axis=0)
        imag = jnp.sum(mine[:, 1] * other[:, 0] - mine[:, 0] * other[:, 1], axis=0)
        pieces.append(jnp.stack([real, imag], axis=1))
    return jnp.stack(pieces, axis=1) * (1.0 / math.sqrt(total_k))


def solution(mesh):
    placed = (P("ka", "ga", None), P(), P())
    return jax.shard_map(
        on_device, mesh=mesh, in_specs=placed, out_specs=P("ka", None, None, "ga"), check_vma=False
    )
```

time: 1010 us -> 238 us (0.24)
  waiting for transfers between devices: 899 us -> 187 us
  starting transfers between devices: 53.1 us -> 20.6 us
  other arithmetic: 21.9 us -> 6.9 us
  local copies, waits for them, and re-layouts: 15.6 us -> 2.52 us
    unnamed x3 -> x1, waiting for transfers between devices: 540 us -> 0.02 us
    ppermute x11 -> x0, waiting for transfers between devices: 203 us -> none  [from_behind(): return lax.ppermute(block, axis, route)]
    all_to_all x0 -> x1, waiting for transfers between devices: none -> 94 us  [on_device(): lax.all_to_all(field.transpose(1, 0, 2, 3), 'ka', 0, 0, tiled=True)]
    psum x1, waiting for transfers between devices: 157 us -> 93 us  [on_device(): rows = lax.psum(picked.astype(jnp.bfloat16), 'ga')]
    ppermute x11 -> x0, starting transfers between devices: 52.9 us -> none  [from_behind(): return lax.ppermute(block, axis, route)]
    all_to_all x0 -> x1, starting transfers between devices: none -> 20.6 us  [on_device(): lax.all_to_all(field.transpose(1, 0, 2, 3), 'ka', 0, 0, tiled=True)]
  transfers between devices with their start and end apart: 13 -> 2, of which waited for: 12 -> 2; matrix products, arithmetic and copies ran while one was open for 1% -> 0% of each run, Pallas kernels for 0% -> 0%
where the time goes in v1:
time: 238 us; the launch traced here: 236 us
  waiting for transfers between devices  187 us (79%)
  starting transfers between devices  20.6 us (9%)
  between operations  17.3 us (7%)
  other arithmetic  6.9 us (3%)
  local copies, waits for them, and re-layouts  2.52 us (1%)
    all_to_all x1, waiting for transfers between devices, on_device(): lax.all_to_all(field.transpose(1, 0, 2, 3), 'ka', 0, 0, tiled=True)  94 us
    psum x1, waiting for transfers between devices, on_device(): rows = lax.psum(picked.astype(jnp.bfloat16), 'ga')  93 us
    all_to_all x1, starting transfers between devices, on_device(): lax.all_to_all(field.transpose(1, 0, 2, 3), 'ka', 0, 0, tiled=True)  20.6 us
  transfers between devices with their start and end apart: 2, of which 2 were waited for; matrix products, arithmetic and copies ran while one was open for 0% of the time, Pallas kernels for 0%

profile of v1, /device:TPU:1, one launch (start us, length us, event | category | flops | bytes accessed | tf_op | source)
XLA Modules:
  0.0 236.4 jit_solution(13524436708039241793)
XLA Ops:
  6.5 0.0 copy-start
  6.5 0.0 all-reduce.2.cloned.1.call-start
  6.5 0.7 broadcast_subtract_fusion
  7.3 0.3 copy-done
  7.6 1.3 fusion.4
  8.9 0.0 all-reduce.2.cloned.1.call-update
  8.9 93.0 %all-reduce.2.cloned.1.call-done = bf16[2,512,256]{2,1,0:T(8,128)(2,1)} async-done(((bf16[2,512,256]{2,1,0:T(8,128)(2,1)}), bf16[2,512,256]{2,1,0:T(8,128)(2,1)}) %all-reduce.2.cloned.1.call-update) | async-done | bytes 524304 | tf_op jit(solution)/shard_map/psum | solution.py:20
  101.9 0.0 copy-start.1
  101.9 1.1 slice_negate_fusion
  103.0 0.1 maximum_bitcast_fusion
  103.1 0.0 copy-done.1
  103.1 0.1 pad_maximum_fusion
  103.2 0.1 copy.5
  103.3 0.7 convolution_convert_fusion
  104.1 1.6 copy.8
  105.6 20.6 %all-to-all-start = ((bf16[64,2,16,512]{3,2,1,0:T(8,128)(2,1)}), bf16[64,2,16,512]{3,2,1,0:T(8,128)(2,1)S(1)}, u32[]{:S(2)}, u32[]{:S(2)}) async-start(bf16[64,2,16,512]{3,2,1,0:T(8,128)(2,1)} %bitcast.26), calls=%async_computation | async-start | bytes 4194304 | tf_op jit(solution)/shard_map/all_to_all | solution.py:28
  126.2 0.0 copy-done.2
  126.2 0.5 fusion.8
  130.5 94.0 %all-to-all-done = bf16[64,2,16,512]{3,2,1,0:T(8,128)(2,1)S(1)} async-done(((bf16[64,2,16,512]{3,2,1,0:T(8,128)(2,1)}), bf16[64,2,16,512]{3,2,1,0:T(8,128)(2,1)S(1)}, u32[]{:S(2)}, u32[]{:S(2)}) %all-to-all-start) | async-done | bytes 2097184 | tf_op jit(solution)/shard_map/all_to_all | solution.py:28
  224.5 0.6 convert_element_type.22
  225.1 1.9 fusion.1
  227.0 1.6 add_reduce_fusion.1
  228.8 0.1 maximum_bitcast_fusion.1
  228.8 0.7 maximum_multiply_fusion
  (5 shorter events, 0.1 us)
Async XLA Ops:
  6.5 1.1 copy-start
  6.5 95.4 %all-reduce.2.cloned.1.call-start = ((), (), s32[]{:S(2)}) async-start(), calls=%async_computation.1 | async-start | bytes 1048576 | tf_op jit(solution)/shard_map/psum | solution.py:20
  101.9 1.2 copy-start.1
  105.6 20.6 %copy-start.2 = (s32[2,128]{1,0:T(2,128)S(1)}, s32[2,128]{1,0:T(2,128)}, u32[]{:S(2)}) copy-start(s32[2,128]{1,0:T(2,128)} %param.4) | copy-start | bytes 3076
  105.6 118.9 %all-to-all-start = ((bf16[64,2,16,512]{3,2,1,0:T(8,128)(2,1)}), bf16[64,2,16,512]{3,2,1,0:T(8,128)(2,1)S(1)}, u32[]{:S(2)}, u32[]{:S(2)}) async-start(bf16[64,2,16,512]{3,2,1,0:T(8,128)(2,1)} %bitcast.26), calls=%async_computation | async-start | bytes 4194304 | tf_op jit(solution)/shard_map/all_to_all | solution.py:28
Sparse Core Ops, SparseCore 0:
  10.3 91.5 all-reduce.1

commit v2 on v1

v2 whole, which is shorter than its diff:
```python
import functools
import math

import jax
import jax.numpy as jnp
from jax import lax
from jax.experimental import pallas as pl
from jax.experimental.pallas import tpu as pltpu
from jax.sharding import PartitionSpec as P

MESH = pl.DeviceIdType.MESH
F32 = jnp.float32
BF16 = jnp.bfloat16


def kernel(
    n_ka, n_ga, scale,
    table_ref, points_ref, orb_ref, out_ref,
    hot, masked, parts, rows, send, recv,
    rs_send, rs_recv, ag_send, ag_recv, x_send, x_recv, own_sem,
):
    kdev, slab, channels = orb_ref.shape
    half = channels // 2
    total_k = kdev * n_ka
    n_z = n_ka // 4
    me, g = lax.axis_index("ka"), lax.axis_index("ga")
    z = me // 4
    zrows = points_ref.shape[0] // n_z
    block = zrows // 4

    barrier = pltpu.get_barrier_semaphore()

    @pl.loop(1, n_ga)
    def _(i):
        pl.semaphore_signal(barrier, inc=1, device_id={"ga": (g + i) % n_ga}, device_id_type=MESH)

    @pl.loop(1, n_ka)
    def _(i):
        pl.semaphore_signal(barrier, inc=1, device_id={"ka": (me + i) % n_ka}, device_id_type=MESH)

    def z_of(b, jz):
        offset = (b + 1) if jz == 0 else (n_z - 1 - b) * (1 - b // (n_ga - 1))
        return (z + offset) % n_z

    grid_row = lax.broadcasted_iota(jnp.int32, (zrows, slab), 1) + g * slab
    for b in range(n_ga):
        for jz in range(2):
            index = points_ref[pl.ds(pl.multiple_of(z_of(b, jz) * zrows, zrows), zrows), :]
            hot[pl.ds((2 * b + jz) * zrows, zrows), :] = (index == grid_row).astype(F32).astype(BF16)
    for k in range(kdev):
        picked = jnp.dot(hot[...], orb_ref[k], preferred_element_type=F32).astype(BF16)
        masked[:, :, k * channels:(k + 1) * channels] = picked.reshape(n_ga, 2 * zrows, channels)

    pl.semaphore_wait(barrier, n_ga - 1 + n_ka - 1)

    @pl.loop(1, n_ga)
    def _(i):
        to = (g + n_ga - i) % n_ga
        pltpu.make_async_remote_copy(
            src_ref=masked.at[to], dst_ref=parts.at[g], send_sem=rs_send, recv_sem=rs_recv,
            device_id={"ga": to}, device_id_type=MESH).start()

    parts[g] = masked[g]
    arrivals = parts.at[pl.ds(0, n_ga - 1)]
    pltpu.make_async_copy(arrivals, arrivals, rs_recv).wait()
    summed = parts[0].astype(F32)
    for i in range(1, n_ga):
        summed = summed + parts[i].astype(F32)
    rows[g] = summed.astype(BF16)

    @pl.loop(1, n_ga)
    def _(i):
        pltpu.make_async_remote_copy(
            src_ref=rows.at[g], dst_ref=rows.at[g], send_sem=ag_send, recv_sem=ag_recv.at[g],
            device_id={"ga": (g + n_ga - i) % n_ga}, device_id_type=MESH).start()

    @pl.loop(0, n_ga)
    def _(i):
        b = (g + i) % n_ga

        @pl.when(i > 0)
        def _():
            pltpu.make_async_copy(rows.at[b], rows.at[b], ag_recv.at[b]).wait()

        for k in range(kdev):
            c = rows[b, :, k * channels:(k + 1) * channels].astype(F32)
            rotated = jnp.concatenate([-c[:, half:], c[:, :half]], axis=1)
            both = jnp.concatenate(
                [c.reshape(8, block, channels), rotated.reshape(8, block, channels)], axis=1)
            left = both.reshape(16 * block, channels).astype(BF16)
            field = lax.dot_general(
                left, orb_ref[k], (((1,), (1,)), ((), ())), preferred_element_type=F32)
            send[b, :, k] = field.astype(BF16).reshape(8, 2 * block, slab)

        for j in range(8):
            to = 4 * z_of(b, j // 4) + j % 4

            @pl.when(to != me)
            def _():
                pltpu.make_async_remote_copy(
                    src_ref=send.at[b, j], dst_ref=recv.at[pl.ds(kdev * me, kdev)],
                    send_sem=x_send, recv_sem=x_recv,
                    device_id={"ka": to}, device_id_type=MESH).start()

            @pl.when(to == me)
            def _():
                pltpu.make_async_copy(
                    send.at[b, j], recv.at[pl.ds(kdev * me, kdev)], own_sem).start()

    def drain(ref, sem):
        pltpu.make_async_copy(ref, ref, sem).wait()

    drain(send.at[0, 0], own_sem)
    drain(recv.at[pl.ds(0, total_k - kdev)], x_recv)

    shifts = [table_ref[q, 0] for q in range(2)]

    def step(k, totals):
        own = recv[k].astype(F32)
        own_re, own_im = own[:block], own[block:]
        new = []
        for q in range(2):
            other = recv[lax.rem(k + shifts[q], total_k)].astype(F32)
            re, im = other[:block], other[block:]
            new.append(totals[2 * q] + (own_re * re + own_im * im))
            new.append(totals[2 * q + 1] + (own_im * re - own_re * im))
        return tuple(new)

    zero = jnp.zeros((block, slab), F32)
    totals = lax.fori_loop(0, total_k, step, (zero,) * 4, unroll=4)
    for i in range(4):
        out_ref[i] = totals[i] * scale

    drain(masked.at[pl.ds(0, n_ga - 1)], rs_send)
    drain(rows.at[pl.ds(0, n_ga - 1)], ag_send)
    drain(recv.at[pl.ds(0, total_k - kdev)], x_send)


def on_device(orbitals, minus_table, points):
    kdev, slab, channels = orbitals.shape
    n_ka, n_ga = lax.axis_size("ka"), lax.axis_size("ga")
    npts = points.shape[0]
    block = npts // n_ka
    total_k = kdev * n_ka
    mine = npts // n_ga
    vmem = pl.BlockSpec(memory_space=pltpu.VMEM)
    dma = pltpu.SemaphoreType.DMA
    out = pl.pallas_call(
        functools.partial(kernel, n_ka, n_ga, 1.0 / math.sqrt(total_k)),
        out_shape=jax.ShapeDtypeStruct((4, block, slab), F32),
        in_specs=[pl.BlockSpec(memory_space=pltpu.SMEM), vmem, vmem],
        out_specs=vmem,
        scratch_shapes=[
            pltpu.VMEM((npts, slab), BF16),
            pltpu.VMEM((n_ga, mine, kdev * channels), BF16),
            pltpu.VMEM((n_ga, mine, kdev * channels), BF16),
            pltpu.VMEM((n_ga, mine, kdev * channels), BF16),
            pltpu.VMEM((n_ga, 8, kdev, 2 * block, slab), BF16),
            pltpu.VMEM((total_k, 2 * block, slab), BF16),
            dma, dma, dma, dma((n_ga,)), dma, dma, dma,
        ],
        compiler_params=pltpu.CompilerParams(
            collective_id=0, has_side_effects=True, vmem_limit_bytes=32 * 1024 * 1024),
    )(minus_table, points.reshape(npts, 1), orbitals)
    return out.reshape(2, 2, block, slab).transpose(2, 0, 1, 3)


def solution(mesh):
    placed = (P("ka", "ga", None), P(), P())
    return jax.shard_map(
        on_device, mesh=mesh, in_specs=placed, out_specs=P("ka", None, None, "ga"), check_vma=False
    )
```

time: 238 us -> 127 us (0.53)
  the two profiles are of different devices: /device:TPU:1 before, /device:TPU:33 now
where the time goes in v2:
time: 127 us; the launch traced here: 126 us
  Pallas kernels  124 us (98%)
  local copies, waits for them, and re-layouts  2.55 us (2%)
    pallas_call x1, Pallas kernels, on_device(): pl.pallas_call(functools.partial(kernel, n_ka, n_ga, 1.0 / math.sqrt(tota...  124 us

profile of v2, /device:TPU:33, one launch (start us, length us, event | category | flops | bytes accessed | tf_op | source)
XLA Modules:
  0.0 126.5 jit_solution(16719572203155360764)
XLA Ops:
  0.0 0.0 copy-start.1
  0.0 0.8 copy.5.points_ref
  0.8 0.0 copy-done.1
  0.9 0.0 copy-start
  0.9 1.0 copy-done
  1.9 123.9 %shard_map.37 = f32[4,8,512]{2,1,0:T(8,128)S(1)} custom-call(s32[2,128]{1,0:T(2,128)S(1)} %copy-done.1, s32[512,1]{1,0:T(8,128)S(1)} %copy.5.points_ref, bf16[2,512,256]{2,1,0:T(8,128)(2,1)S(1)} %copy-done), custom_call_target="tpu_custom_call" | custom-call | tf_op jit(solution)/shard_map/pallas_call | solution.py:148
  125.8 0.7 copy.8
Async XLA Ops:
  0.0 0.8 copy-start.1
  0.9 1.0 copy-start

commit v3 on v1

v3 whole, which is shorter than its diff:
```python
import functools
import math

import jax
import jax.numpy as jnp
from jax import lax
from jax.experimental import pallas as pl
from jax.experimental.pallas import tpu as pltpu
from jax.sharding import PartitionSpec as P

MESH = pl.DeviceIdType.MESH
F32 = jnp.float32
BF16 = jnp.bfloat16
NZ, NX, NY = 16, 4, 4
PLANE = NX * NY


def kernel(
    scale,
    table_ref, points_ref, orb_ref, out_ref,
    hot, masked, parts, rows, grid, fields, stage, tiles, got,
    rs_send, rs_recv, grid_send, grid_recv, gridx_send, rows_send, rows_recv, rowsy_send,
    pair_send, pair_recv, tile_send, tile_recv,
):
    kdev, slab, channels = orb_ref.shape
    half = channels // 2
    chunk = slab // NZ
    total_k = kdev * 4 * NZ
    me, g = lax.axis_index("ka"), lax.axis_index("ga")
    z, x_hi, core = me // 4, (me // 2) % 2, me % 2
    y, x_lo = g // 2, g % 2
    x = 2 * x_hi + x_lo
    place = x * NY + y
    in_turn = (1 - (z // 8 - x_lo) ** 2) * (1 - (core - x_lo) ** 2)

    def in_plane(xx, yy):
        return {"ka": 4 * z + 2 * (xx // 2) + core, "ga": 2 * yy + xx % 2}

    def send(src, dst, send_sem, recv_sem, to):
        pltpu.make_async_remote_copy(
            src_ref=src, dst_ref=dst, send_sem=send_sem, recv_sem=recv_sem,
            device_id=to, device_id_type=MESH).start()

    def drain(ref, sem):
        pltpu.make_async_copy(ref, ref, sem).wait()

    barrier = pltpu.get_barrier_semaphore()

    def greet(to):
        pl.semaphore_signal(barrier, inc=1, device_id=to, device_id_type=MESH)

    @pl.loop(1, NZ)
    def _(i):
        greet({"ka": (me + 4 * i) % (4 * NZ)})

    @pl.loop(1, PLANE)
    def _(i):
        to = (place + i) % PLANE
        greet(in_plane(to // NY, to % NY))

    greet({"ka": me + 1 - 2 * core})

    @pl.loop(0, NZ)
    def _(zz):
        @pl.when((in_turn == 0) | (zz != z))
        def _():
            greet({"ka": 4 * zz + 2 * x_hi + x_lo, "ga": 2 * y + z // 8})

    grid_row = lax.broadcasted_iota(jnp.int32, hot.shape, 0) + g * slab
    hot[...] = (points_ref[...] == grid_row).astype(F32).astype(BF16)
    for k in range(kdev):
        picked = lax.dot_general(
            hot[...], orb_ref[k], (((0,), (0,)), ((), ())), preferred_element_type=F32)
        masked[:, :, :, :, k * channels:(k + 1) * channels] = picked.astype(BF16).reshape(
            masked.shape[:4] + (channels,))

    pl.semaphore_wait(barrier, (NZ - 1) + (PLANE - 1) + 1 + NZ - in_turn)

    @pl.loop(1, PLANE)
    def _(i):
        to = (place + i) % PLANE
        xx, yy = to // NY, to % NY
        send(masked.at[4 * (xx % 2) + yy, :, xx // 2], parts.at[place],
             rs_send, rs_recv, in_plane(xx, yy))

    @pl.loop(1, NZ)
    def _(i):
        zz = (z + NZ + ((i + 1) // 2) * (2 * (i % 2) - 1)) % NZ
        send(orb_ref.at[:, pl.ds(pl.multiple_of(chunk * zz, chunk), chunk)], grid.at[x, z],
             grid_send, grid_recv.at[x, z], {"ka": 4 * zz + me % 4})

    def spread_grid(zz):
        @pl.loop(1, NX)
        def _(i):
            send(grid.at[x, zz], grid.at[x, zz], gridx_send, grid_recv.at[x, zz],
                 in_plane((x + i) % NX, y))

    def spread_rows(zz):
        @pl.loop(1, NY)
        def _(i):
            send(rows.at[y, zz], rows.at[y, zz], rowsy_send, rows_recv.at[y, zz],
                 in_plane(x, (y + i) % NY))

    def pass_rows(zz, to):
        send(rows.at[y, zz], rows.at[y, zz], rows_send, rows_recv.at[y, zz],
             {"ka": 4 * ((to + NZ) % NZ) + me % 4})

    grid[x, z] = orb_ref[:, pl.ds(pl.multiple_of(chunk * z, chunk), chunk), :]
    spread_grid(z)

    parts[place] = masked[4 * x_lo + y, :, x_hi]
    drain(parts.at[pl.ds(0, PLANE - 1)], rs_recv)
    for h in range(2):
        summed = parts[8 * h].astype(F32)
        for i in range(1, 8):
            summed = summed + parts[8 * h + i].astype(F32)
        rows[y, z, h] = summed.astype(BF16)
    pass_rows(z, z + 1)
    pass_rows(z, z - 1)
    spread_rows(z)

    @pl.loop(1, NZ // 2 + 1)
    def _(t):
        down = (z + NZ - t) % NZ
        drain(rows.at[y, down], rows_recv.at[y, down])

        @pl.when(t < NZ // 2)
        def _():
            pass_rows(down, z + 1)

        spread_rows(down)
        up = (z + t) % NZ

        @pl.when(t < NZ // 2)
        def _():
            drain(rows.at[y, up], rows_recv.at[y, up])

            @pl.when(t < NZ // 2 - 1)
            def _():
                pass_rows(up, z - 1)

            spread_rows(up)

        drain(grid.at[x, down], grid_recv.at[x, down])
        spread_grid(down)

        @pl.when(t < NZ // 2)
        def _():
            drain(grid.at[x, up], grid_recv.at[x, up])
            spread_grid(up)

    @pl.loop(0, NZ)
    def _(i):
        zz = (z + NZ + ((i + 1) // 2) * (2 * (i % 2) - 1)) % NZ

        @pl.loop(1, NX)
        def _(j):
            xx = (x + j) % NX
            drain(grid.at[xx, zz], grid_recv.at[xx, zz])

        @pl.loop(1, NY)
        def _(j):
            yy = (y + j) % NY
            drain(rows.at[yy, zz], rows_recv.at[yy, zz])

        for h in range(2):
            for k in range(kdev):
                picked = rows[:, zz, h, :, :, k * channels:(k + 1) * channels].reshape(
                    NY * 32, channels)
                stack = []
                for lo in (core, 1 - core):
                    phi = grid[2 * h + lo, zz, k]
                    stack += [phi, jnp.concatenate([phi[:, half:], -phi[:, :half]], axis=1)]
                field = lax.dot_general(
                    jnp.concatenate(stack, axis=0), picked, (((1,), (1,)), ((), ())),
                    preferred_element_type=F32).astype(BF16)
                fields[8 * zz + 4 * h + 2 * core + k] = field[:2 * chunk]
                stage[zz, h, k] = field[2 * chunk:]
            send(stage.at[zz, h], fields.at[pl.ds(8 * zz + 4 * h + 2 * core, kdev)],
                 pair_send, pair_recv, {"ka": me + 1 - 2 * core})

    drain(stage, pair_recv)

    shifts = [table_ref[q, 0] for q in range(2)]

    def step(k, totals):
        own = fields[k].astype(F32)
        own_re, own_im = own[:chunk], own[chunk:]
        new = []
        for q in range(2):
            other = fields[lax.rem(k + shifts[q], total_k)].astype(F32)
            re, im = other[:chunk], other[chunk:]
            new.append(totals[2 * q] + (own_re * re + own_im * im))
            new.append(totals[2 * q + 1] + (own_im * re - own_re * im))
        return tuple(new)

    zero = jnp.zeros((chunk, 128), F32)
    totals = lax.fori_loop(0, total_k, step, (zero,) * 4, unroll=4)
    tiles[...] = (jnp.concatenate(totals, axis=0) * scale).T.reshape(tiles.shape)

    @pl.loop(0, 16)
    def _(j):
        zz, cc = 8 * x_lo + j // 2, j % 2
        stays = (in_turn == 1) & (zz == z) & (cc == core)

        @pl.when(stays)
        def _():
            pltpu.make_async_copy(tiles.at[j], got.at[z], tile_recv).start()

        @pl.when(jnp.logical_not(stays))
        def _():
            send(tiles.at[j], got.at[z], tile_send, tile_recv,
                 {"ka": 4 * zz + 2 * x_hi + cc, "ga": 2 * y + core})

    drain(got, tile_recv)
    for i in range(4):
        out_ref[i] = jnp.concatenate(
            [got[zz, :, chunk * i:chunk * (i + 1)] for zz in range(NZ)], axis=1)

    drain(parts.at[pl.ds(0, PLANE - 1)], rs_send)
    drain(grid.at[0, pl.ds(0, NZ - 1)], grid_send)
    drain(grid.at[pl.ds(0, NX - 1)], gridx_send)
    drain(rows.at[0, pl.ds(0, NZ - 1)], rows_send)
    drain(rows.at[pl.ds(0, NY - 1)], rowsy_send)
    drain(stage, pair_send)

    @pl.when(in_turn == 1)
    def _():
        drain(tiles.at[pl.ds(0, 15)], tile_send)

    @pl.when(in_turn == 0)
    def _():
        drain(tiles, tile_send)


def on_device(orbitals, minus_table, points):
    kdev, slab, channels = orbitals.shape
    npts = points.shape[0]
    total_k = kdev * 4 * NZ
    chunk = slab // NZ
    wide = kdev * channels
    vmem = pl.BlockSpec(memory_space=pltpu.VMEM)
    dma = pltpu.SemaphoreType.DMA
    out = pl.pallas_call(
        functools.partial(kernel, 1.0 / math.sqrt(total_k)),
        out_shape=jax.ShapeDtypeStruct((4, 8, slab), F32),
        in_specs=[pl.BlockSpec(memory_space=pltpu.SMEM), vmem, vmem],
        out_specs=vmem,
        scratch_shapes=[
            pltpu.VMEM((slab, npts), BF16),
            pltpu.VMEM((8, 2, 2, 16, wide), BF16),
            pltpu.VMEM((PLANE, 2, 16, wide), BF16),
            pltpu.VMEM((NY, NZ, 2, 2, 16, wide), BF16),
            pltpu.VMEM((NX, NZ, kdev, chunk, channels), BF16),
            pltpu.VMEM((total_k, 2 * chunk, 128), BF16),
            pltpu.VMEM((NZ, 2, kdev, 2 * chunk, 128), BF16),
            pltpu.VMEM((16, 8, 128), F32),
            pltpu.VMEM((NZ, 8, 128), F32),
            dma, dma, dma, dma((NX, NZ)), dma, dma, dma((NY, NZ)), dma,
            dma, dma, dma, dma,
        ],
        compiler_params=pltpu.CompilerParams(
            collective_id=0, has_side_effects=True, vmem_limit_bytes=40 * 1024 * 1024),
    )(minus_table, points.reshape(1, npts), orbitals)
    return out.reshape(2, 2, 8, slab).transpose(2, 0, 1, 3)


def solution(mesh):
    placed = (P("ka", "ga", None), P(), P())
    return jax.shard_map(
        on_device, mesh=mesh, in_specs=placed, out_specs=P("ka", None, None, "ga"), check_vma=False
    )
```

time: 238 us -> 101 us (0.42)
  waiting for transfers between devices: 187 us -> 0 us
  Pallas kernels: 0 us -> 98 us
  starting transfers between devices: 20.6 us -> 0 us
  between operations: 17.3 us -> 0.01 us
  other arithmetic: 6.9 us -> 0 us
    pallas_call x0 -> x1, Pallas kernels: none -> 98 us  [on_device(): pl.pallas_call(functools.partial(kernel, 1.0 / math.sqrt(total_k)), out_s...]
    all_to_all x1 -> x0, waiting for transfers between devices: 94 us -> none  [on_device(): lax.all_to_all(field.transpose(1, 0, 2, 3), 'ka', 0, 0, tiled=True)]
    psum x1 -> x0, waiting for transfers between devices: 93 us -> none  [on_device(): rows = lax.psum(picked.astype(jnp.bfloat16), 'ga')]
    all_to_all x1 -> x0, starting transfers between devices: 20.6 us -> none  [on_device(): lax.all_to_all(field.transpose(1, 0, 2, 3), 'ka', 0, 0, tiled=True)]
    convert_element_type x2 -> x0, other arithmetic: 2.48 us -> none  [the longest x1 1.91 us: on_device(): lax.dynamic_slice_in_dim(twice, minus_table[transfer, 0], total_k, 0)]
  transfers between devices with their start and end apart: 2 -> 0, of which waited for: 2 -> 0; matrix products, arithmetic and copies ran while one was open for 0% -> 0% of each run, Pallas kernels for 0% -> 0%
where the time goes in v3:
time: 101 us
  Pallas kernels  98 us (97%)
  local copies, waits for them, and re-layouts  3.08 us (3%)
    pallas_call x1, Pallas kernels, on_device(): pl.pallas_call(functools.partial(kernel, 1.0 / math.sqrt(total_k)), out_s...  98 us
    unnamed x6, local copies, waits for them, and re-layouts  2.4 us

profile of v3, /device:TPU:1, one launch (start us, length us, event | category | flops | bytes accessed | tf_op | source)
XLA Modules:
  0.0 101.0 jit_solution(7582649885906717241)
XLA Ops:
  0.0 0.0 copy-start.2
  0.0 0.7 copy-done.2
  0.7 0.0 copy-start
  0.7 1.0 %copy-done = bf16[2,512,256]{2,1,0:T(8,128)(2,1)S(1)} copy-done((bf16[2,512,256]{2,1,0:T(8,128)(2,1)S(1)}, bf16[2,512,256]{2,1,0:T(8,128)(2,1)}, u32[]{:S(2)}) %copy-start) | copy-done | bytes 524312
  1.7 0.0 copy-start.1
  1.7 0.7 copy-done.1
  2.4 98.0 %shard_map.37 = f32[4,8,512]{2,1,0:T(8,128)S(1)} custom-call(s32[2,128]{1,0:T(2,128)S(1)} %copy-done.2, s32[1,512]{1,0:T(1,128)S(1)} %bitcast.6, bf16[2,512,256]{2,1,0:T(8,128)(2,1)S(1)} %copy-done), custom_call_target="tpu_custom_call" | custom-call | tf_op jit(solution)/shard_map/pallas_call | solution.py:244
  100.4 0.7 copy.6
Async XLA Ops:
  0.0 0.7 copy-start.2
  0.7 1.0 %copy-start = (bf16[2,512,256]{2,1,0:T(8,128)(2,1)S(1)}, bf16[2,512,256]{2,1,0:T(8,128)(2,1)}, u32[]{:S(2)}) copy-start(bf16[2,512,256]{2,1,0:T(8,128)(2,1)} %orb_ref.1) | copy-start | bytes 1572868
  1.7 0.7 copy-start.1

commit v4 on v3

v4 whole, which is shorter than its diff:
```python
import functools
import math

import jax
import jax.numpy as jnp
from jax import lax
from jax.experimental import pallas as pl
from jax.experimental.pallas import tpu as pltpu
from jax.sharding import PartitionSpec as P

MESH = pl.DeviceIdType.MESH
F32 = jnp.float32
BF16 = jnp.bfloat16
NZ, NX, NY = 16, 4, 4
PLANE = NX * NY
LAG = 4
EARLY = 10


def kernel(
    scale,
    table_ref, points_ref, orbitals_ref, out_ref,
    orb_ref, hot, masked, parts, rows, grid, fields, stage, tiles, got,
    rs_send, rs_recv, grid_send, grid_recv, gridx_send, rows_send, rows_recv, rowsy_send,
    pair_send, pair_recv, tile_send, tile_recv, orb_sem,
):
    kdev, slab, channels = orb_ref.shape
    half = channels // 2
    chunk = slab // NZ
    total_k = kdev * 4 * NZ
    me, g = lax.axis_index("ka"), lax.axis_index("ga")
    z, x_hi, core = me // 4, (me // 2) % 2, me % 2
    y, x_lo = g // 2, g % 2
    x = 2 * x_hi + x_lo
    place = x * NY + y
    in_turn = (1 - (z // 8 - x_lo) ** 2) * (1 - (core - x_lo) ** 2)

    def in_plane(xx, yy):
        return {"ka": 4 * z + 2 * (xx // 2) + core, "ga": 2 * yy + xx % 2}

    def send(src, dst, send_sem, recv_sem, to):
        pltpu.make_async_remote_copy(
            src_ref=src, dst_ref=dst, send_sem=send_sem, recv_sem=recv_sem,
            device_id=to, device_id_type=MESH).start()

    def drain(ref, sem):
        pltpu.make_async_copy(ref, ref, sem).wait()

    fetch = pltpu.make_async_copy(orbitals_ref, orb_ref, orb_sem)
    fetch.start()
    barrier = pltpu.get_barrier_semaphore()

    def greet(to):
        pl.semaphore_signal(barrier, inc=1, device_id=to, device_id_type=MESH)

    @pl.loop(1, NZ)
    def _(i):
        greet({"ka": (me + 4 * i) % (4 * NZ)})

    @pl.loop(1, PLANE)
    def _(i):
        to = (place + i) % PLANE
        greet(in_plane(to // NY, to % NY))

    greet({"ka": me + 1 - 2 * core})

    @pl.loop(0, NZ)
    def _(zz):
        @pl.when((in_turn == 0) | (zz != z))
        def _():
            greet({"ka": 4 * zz + 2 * x_hi + x_lo, "ga": 2 * y + z // 8})

    index = jnp.broadcast_to(points_ref[...].astype(F32), (128, points_ref.shape[1])).T
    lane = lax.broadcasted_iota(jnp.int32, index.shape, 1) + g * slab
    for first in range(0, slab, 128):
        hot[:, first:first + 128] = (index == (lane + first).astype(F32)).astype(F32).astype(BF16)
    fetch.wait()
    for k in range(kdev):
        picked = jnp.dot(hot[...], orb_ref[k], preferred_element_type=F32)
        masked[k] = picked.astype(BF16).reshape(masked.shape[1:])

    pl.semaphore_wait(barrier, (NZ - 1) + (PLANE - 1) + 1 + NZ - in_turn)

    for k in range(kdev):
        @pl.loop(1, PLANE)
        def _(i):
            to = (place + i) % PLANE
            xx, yy = to // NY, to % NY
            send(masked.at[k, 4 * (xx % 2) + yy, :, xx // 2], parts.at[k, place],
                 rs_send, rs_recv.at[k], in_plane(xx, yy))

    def ship_grid(distance, k):
        for step in (distance, NZ - distance)[:2 if distance < NZ // 2 else 1]:
            zz = (z + step) % NZ
            send(orb_ref.at[k, pl.ds(pl.multiple_of(chunk * zz, chunk), chunk)], grid.at[x, z, k],
                 grid_send, grid_recv.at[x, z], {"ka": 4 * zz + me % 4})

    ships = [(distance, k) for distance in range(1, NZ // 2 + 1) for k in range(kdev)]
    for ship in ships[:EARLY]:
        ship_grid(*ship)

    def spread_grid(zz):
        @pl.loop(1, NX)
        def _(i):
            send(grid.at[x, zz], grid.at[x, zz], gridx_send, grid_recv.at[x, zz],
                 in_plane((x + i) % NX, y))

    def hand_rows(yy, zz, k, send_sem, to):
        send(rows.at[yy, zz, k], rows.at[yy, zz, k], send_sem, rows_recv.at[yy, zz, k], to)

    def wait_rows(yy, zz, k):
        drain(rows.at[yy, zz, k], rows_recv.at[yy, zz, k])

    def spread_rows(zz, k):
        for to in (1, NY - 1):
            hand_rows(y, zz, k, rowsy_send, in_plane(x, (y + to) % NY))

    def relay_rows(zz, k):
        source = (y + NY - 1 + 2 * (zz % 2)) % NY
        wait_rows(source, zz, k)
        hand_rows(source, zz, k, rowsy_send, in_plane(x, (y + 1 + 2 * (zz % 2)) % NY))

    def pass_rows(zz, k, to):
        hand_rows(y, zz, k, rows_send, {"ka": 4 * ((to + NZ) % NZ) + me % 4})

    def make_fields(zz):
        @pl.loop(1, NX)
        def _(j):
            xx = (x + j) % NX
            drain(grid.at[xx, zz], grid_recv.at[xx, zz])

        for yy in ((y + 1 + 2 * (zz % 2)) % NY, (y + 2) % NY):
            for k in range(kdev):
                wait_rows(yy, zz, k)
        for h in range(2):
            for k in range(kdev):
                picked = rows[:, zz, k, h].reshape(NY * 32, channels)
                stack = []
                for lo in (core, 1 - core):
                    phi = grid[2 * h + lo, zz, k]
                    stack += [phi, jnp.concatenate([phi[:, half:], -phi[:, :half]], axis=1)]
                field = lax.dot_general(
                    jnp.concatenate(stack, axis=0), picked, (((1,), (1,)), ((), ())),
                    preferred_element_type=F32).astype(BF16)
                fields[8 * zz + 4 * h + 2 * core + k] = field[:2 * chunk]
                stage[zz, h, k] = field[2 * chunk:]
            send(stage.at[zz, h], fields.at[pl.ds(8 * zz + 4 * h + 2 * core, kdev)],
                 pair_send, pair_recv, {"ka": me + 1 - 2 * core})

    grid[x, z] = orb_ref[:, pl.ds(pl.multiple_of(chunk * z, chunk), chunk), :]
    spread_grid(z)

    for k in range(kdev):
        parts[k, place] = masked[k, 4 * x_lo + y, :, x_hi]
        drain(parts.at[k, pl.ds(0, PLANE - 1)], rs_recv.at[k])
        for h in range(2):
            summed = parts[k, 8 * h].astype(F32)
            for i in range(1, 8):
                summed = summed + parts[k, 8 * h + i].astype(F32)
            rows[y, z, k, h] = summed.astype(BF16)
        pass_rows(z, k, z + 1)
        pass_rows(z, k, z - 1)
        spread_rows(z, k)
    for ship in ships[EARLY:EARLY + 1]:
        ship_grid(*ship)

    def both_ways(distance):
        return [(z + NZ - distance) % NZ, (z + distance) % NZ][:1 + (0 < distance < NZ // 2)]

    for t in range(1, NZ // 2 + 1):
        for k in range(kdev):
            for zz, ahead in zip(both_ways(t), (1, -1)):
                wait_rows(y, zz, k)
                if t < NZ // 2 - (ahead < 0):
                    pass_rows(zz, k, z + ahead)
                spread_rows(zz, k)
        for ship in ships[EARLY + t:EARLY + t + 1]:
            ship_grid(*ship)
        for zz in both_ways(t):
            drain(grid.at[x, zz], grid_recv.at[x, zz])
            spread_grid(zz)
        if t >= 2:
            for k in range(kdev):
                for zz in both_ways(t - 2):
                    relay_rows(zz, k)
        if t >= LAG:
            for zz in both_ways(t - LAG):
                make_fields(zz)
    for distance in (NZ // 2 - 1, NZ // 2):
        for k in range(kdev):
            for zz in both_ways(distance):
                relay_rows(zz, k)
    for distance in range(NZ // 2 + 1 - LAG, NZ // 2 + 1):
        for zz in both_ways(distance):
            make_fields(zz)

    drain(stage, pair_recv)

    shifts = [table_ref[q, 0] for q in range(2)]

    def step(k, totals):
        own = fields[k].astype(F32)
        own_re, own_im = own[:chunk], own[chunk:]
        new = []
        for q in range(2):
            other = fields[lax.rem(k + shifts[q], total_k)].astype(F32)
            re, im = other[:chunk], other[chunk:]
            new.append(totals[2 * q] + (own_re * re + own_im * im))
            new.append(totals[2 * q + 1] + (own_im * re - own_re * im))
        return tuple(new)

    zero = jnp.zeros((chunk, 128), F32)
    totals = lax.fori_loop(0, total_k, step, (zero,) * 4, unroll=4)
    tiles[...] = (jnp.concatenate(totals, axis=0) * scale).T.reshape(tiles.shape)

    @pl.loop(0, 16)
    def _(j):
        zz, cc = 8 * x_lo + j // 2, j % 2
        stays = (in_turn == 1) & (zz == z) & (cc == core)

        @pl.when(stays)
        def _():
            pltpu.make_async_copy(tiles.at[j], got.at[z], tile_recv).start()

        @pl.when(jnp.logical_not(stays))
        def _():
            send(tiles.at[j], got.at[z], tile_send, tile_recv,
                 {"ka": 4 * zz + 2 * x_hi + cc, "ga": 2 * y + core})

    drain(got, tile_recv)
    for i in range(4):
        out_ref[i] = jnp.concatenate(
            [got[zz, :, chunk * i:chunk * (i + 1)] for zz in range(NZ)], axis=1)

    drain(parts.at[:, pl.ds(0, PLANE - 1)], rs_send)
    drain(grid.at[0, pl.ds(0, NZ - 1)], grid_send)
    drain(grid.at[pl.ds(0, NX - 1)], gridx_send)
    drain(rows.at[0, pl.ds(0, NZ - 1)], rows_send)
    drain(rows.at[pl.ds(0, NY - 1)], rowsy_send)
    drain(stage, pair_send)

    @pl.when(in_turn == 1)
    def _():
        drain(tiles.at[pl.ds(0, 15)], tile_send)

    @pl.when(in_turn == 0)
    def _():
        drain(tiles, tile_send)


def on_device(orbitals, minus_table, points):
    kdev, slab, channels = orbitals.shape
    npts = points.shape[0]
    total_k = kdev * 4 * NZ
    chunk = slab // NZ
    vmem = pl.BlockSpec(memory_space=pltpu.VMEM)
    dma = pltpu.SemaphoreType.DMA
    out = pl.pallas_call(
        functools.partial(kernel, 1.0 / math.sqrt(total_k)),
        out_shape=jax.ShapeDtypeStruct((4, 8, slab), F32),
        in_specs=[pl.BlockSpec(memory_space=pltpu.SMEM), vmem, pl.BlockSpec(memory_space=pl.ANY)],
        out_specs=vmem,
        scratch_shapes=[
            pltpu.VMEM((kdev, slab, channels), BF16),
            pltpu.VMEM((npts, slab), BF16),
            pltpu.VMEM((kdev, 8, 2, 2, 16, channels), BF16),
            pltpu.VMEM((kdev, PLANE, 2, 16, channels), BF16),
            pltpu.VMEM((NY, NZ, kdev, 2, 2, 16, channels), BF16),
            pltpu.VMEM((NX, NZ, kdev, chunk, channels), BF16),
            pltpu.VMEM((total_k, 2 * chunk, 128), BF16),
            pltpu.VMEM((NZ, 2, kdev, 2 * chunk, 128), BF16),
            pltpu.VMEM((16, 8, 128), F32),
            pltpu.VMEM((NZ, 8, 128), F32),
            dma, dma((kdev,)), dma, dma((NX, NZ)), dma, dma, dma((NY, NZ, kdev)), dma,
            dma, dma, dma, dma, dma,
        ],
        compiler_params=pltpu.CompilerParams(
            collective_id=0, has_side_effects=True, vmem_limit_bytes=60 * 1024 * 1024),
    )(minus_table, points.reshape(1, npts), orbitals)
    return out.reshape(2, 2, 8, slab).transpose(2, 0, 1, 3)


def solution(mesh):
    placed = (P("ka", "ga", None), P(), P())
    return jax.shard_map(
        on_device, mesh=mesh, in_specs=placed, out_specs=P("ka", None, None, "ga"), check_vma=False
    )
```

time: 101 us -> 82.2 us (0.81)
  Pallas kernels: 98 us -> 80.3 us
  local copies, waits for them, and re-layouts: 3.08 us -> 1.52 us
    pallas_call x1, Pallas kernels: 98 us -> 80.3 us  [on_device(): pl.pallas_call(functools.partial(kernel, 1.0 / math.sqrt(total_k)), out_s...]
    unnamed x6 -> x0, local copies, waits for them, and re-layouts: 2.4 us -> none
where the time goes in v4:
time: 82.2 us; the launch traced here: 81.8 us
  Pallas kernels  80.3 us (98%)
  local copies, waits for them, and re-layouts  1.52 us (2%)
    pallas_call x1, Pallas kernels, on_device(): pl.pallas_call(functools.partial(kernel, 1.0 / math.sqrt(total_k)), out_s...  80.3 us

profile of v4, /device:TPU:1, one launch (start us, length us, event | category | flops | bytes accessed | tf_op | source)
XLA Modules:
  0.0 81.8 jit_solution(9755840063291330111)
XLA Ops:
  0.0 80.3 %shard_map.37 = f32[4,8,512]{2,1,0:T(8,128)} custom-call(s32[2,128]{1,0:T(2,128)} %table_ref.1, s32[1,512]{1,0:T(1,128)} %bitcast.6, bf16[2,512,256]{2,1,0:T(8,128)(2,1)} %orbitals_ref.1), custom_call_target="tpu_custom_call" | custom-call | tf_op jit(solution)/shard_map/pallas_call | solution.py:258
  80.3 1.5 %copy.6 = f32[2,2,8,512]{3,1,0,2:T(2,128)} copy(f32[2,2,8,512]{3,2,1,0:T(8,128)} %bitcast.5) | data formatting | bytes 131072 | tf_op jit(solution)/shard_map/reshape | solution.py:280

commit v5 on v4

--- a/solution.py
+++ b/solution.py
@@ -14,7 +14,7 @@
 NZ, NX, NY = 16, 4, 4
 PLANE = NX * NY
 LAG = 4
-EARLY = 10
+EARLY = 9
 
 
 def kernel(
@@ -53,9 +53,20 @@
     def greet(to):
         pl.semaphore_signal(barrier, inc=1, device_id=to, device_id_type=MESH)
 
-    @pl.loop(1, NZ)
+    def far_first(i):
+        return (z + NZ // 2 + ((i + 1) // 2) * (2 * (i % 2) - 1) + NZ) % NZ
+
+    @pl.loop(0, NZ)
     def _(i):
-        greet({"ka": (me + 4 * i) % (4 * NZ)})
+        zz = far_first(i)
+
+        @pl.when((in_turn == 0) | (zz != z))
+        def _():
+            greet({"ka": 4 * zz + 2 * x_hi + x_lo, "ga": 2 * y + z // 8})
+
+        @pl.when(zz != z)
+        def _():
+            greet({"ka": 4 * zz + me % 4})
 
     @pl.loop(1, PLANE)
     def _(i):
@@ -63,12 +74,6 @@
         greet(in_plane(to // NY, to % NY))
 
     greet({"ka": me + 1 - 2 * core})
-
-    @pl.loop(0, NZ)
-    def _(zz):
-        @pl.when((in_turn == 0) | (zz != z))
-        def _():
-            greet({"ka": 4 * zz + 2 * x_hi + x_lo, "ga": 2 * y + z // 8})
 
     index = jnp.broadcast_to(points_ref[...].astype(F32), (128, points_ref.shape[1])).T
     lane = lax.broadcasted_iota(jnp.int32, index.shape, 1) + g * slab
@@ -116,9 +121,9 @@
             hand_rows(y, zz, k, rowsy_send, in_plane(x, (y + to) % NY))
 
     def relay_rows(zz, k):
-        source = (y + NY - 1 + 2 * (zz % 2)) % NY
+        source = (y + NY - 1 + 2 * (k % 2)) % NY
         wait_rows(source, zz, k)
-        hand_rows(source, zz, k, rowsy_send, in_plane(x, (y + 1 + 2 * (zz % 2)) % NY))
+        hand_rows(source, zz, k, rowsy_send, in_plane(x, (y + 1 + 2 * (k % 2)) % NY))
 
     def pass_rows(zz, k, to):
         hand_rows(y, zz, k, rows_send, {"ka": 4 * ((to + NZ) % NZ) + me % 4})
@@ -129,9 +134,9 @@
             xx = (x + j) % NX
             drain(grid.at[xx, zz], grid_recv.at[xx, zz])
 
-        for yy in ((y + 1 + 2 * (zz % 2)) % NY, (y + 2) % NY):
-            for k in range(kdev):
-                wait_rows(yy, zz, k)
+        for k in range(kdev):
+            wait_rows((y + 1 + 2 * (k % 2)) % NY, zz, k)
+            wait_rows((y + 2) % NY, zz, k)
         for h in range(2):
             for k in range(kdev):
                 picked = rows[:, zz, k, h].reshape(NY * 32, channels)
@@ -179,19 +184,17 @@
         for zz in both_ways(t):
             drain(grid.at[x, zz], grid_recv.at[x, zz])
             spread_grid(zz)
-        if t >= 2:
-            for k in range(kdev):
-                for zz in both_ways(t - 2):
-                    relay_rows(zz, k)
+        for k in range(kdev):
+            for zz in both_ways(t - 1):
+                relay_rows(zz, k)
         if t >= LAG:
             for zz in both_ways(t - LAG):
                 make_fields(zz)
-    for distance in (NZ // 2 - 1, NZ // 2):
-        for k in range(kdev):
-            for zz in both_ways(distance):
+    for t in range(NZ // 2 + 1, NZ // 2 + 1 + LAG):
+        for k in range(kdev):
+            for zz in both_ways(t - 1) if t < NZ // 2 + 2 else ():
                 relay_rows(zz, k)
-    for distance in range(NZ // 2 + 1 - LAG, NZ // 2 + 1):
-        for zz in both_ways(distance):
+        for zz in both_ways(t - LAG):
             make_fields(zz)
 
     drain(stage, pair_recv)
@@ -210,7 +213,7 @@
         return tuple(new)
 
     zero = jnp.zeros((chunk, 128), F32)
-    totals = lax.fori_loop(0, total_k, step, (zero,) * 4, unroll=4)
+    totals = lax.fori_loop(0, total_k, step, (zero,) * 4, unroll=8)
     tiles[...] = (jnp.concatenate(totals, axis=0) * scale).T.reshape(tiles.shape)
 
     @pl.loop(0, 16)

time: 82.2 us -> 80.6 us (0.981); the launches traced: 81.8 us -> 79.3 us
  Pallas kernels: 80.3 us -> 77.7 us
    pallas_call x1, Pallas kernels: 80.3 us -> 77.7 us  [on_device(): pl.pallas_call(functools.partial(kernel, 1.0 / math.sqrt(total_k)), out_s...]
where the time goes in v5:
time: 80.6 us; the launch traced here: 79.3 us
  Pallas kernels  77.7 us (96%)
  local copies, waits for them, and re-layouts  1.52 us (2%)
    pallas_call x1, Pallas kernels, on_device(): pl.pallas_call(functools.partial(kernel, 1.0 / math.sqrt(total_k)), out_s...  77.7 us

profile of v5, /device:TPU:1, one launch (start us, length us, event | category | flops | bytes accessed | tf_op | source)
XLA Modules:
  0.0 79.3 jit_solution(19006187218794279)
XLA Ops:
  0.0 77.7 %shard_map.37 = f32[4,8,512]{2,1,0:T(8,128)} custom-call(s32[2,128]{1,0:T(2,128)} %table_ref.1, s32[1,512]{1,0:T(1,128)} %bitcast.6, bf16[2,512,256]{2,1,0:T(8,128)(2,1)} %orbitals_ref.1), custom_call_target="tpu_custom_call" | custom-call | tf_op jit(solution)/shard_map/pallas_call | solution.py:261
  77.8 1.5 %copy.6 = f32[2,2,8,512]{3,1,0,2:T(2,128)} copy(f32[2,2,8,512]{3,2,1,0:T(8,128)} %bitcast.5) | data formatting | bytes 131072 | tf_op jit(solution)/shard_map/reshape | solution.py:283

commit v6 on v5

--- a/solution.py
+++ b/solution.py
@@ -86,13 +86,15 @@
 
     pl.semaphore_wait(barrier, (NZ - 1) + (PLANE - 1) + 1 + NZ - in_turn)
 
-    for k in range(kdev):
+    def ship_masked(k):
         @pl.loop(1, PLANE)
         def _(i):
             to = (place + i) % PLANE
             xx, yy = to // NY, to % NY
             send(masked.at[k, 4 * (xx % 2) + yy, :, xx // 2], parts.at[k, place],
-                 rs_send, rs_recv.at[k], in_plane(xx, yy))
+                 rs_send.at[k], rs_recv.at[k], in_plane(xx, yy))
+
+    ship_masked(0)
 
     def ship_grid(distance, k):
         for step in (distance, NZ - distance)[:2 if distance < NZ // 2 else 1]:
@@ -103,6 +105,8 @@
     ships = [(distance, k) for distance in range(1, NZ // 2 + 1) for k in range(kdev)]
     for ship in ships[:EARLY]:
         ship_grid(*ship)
+
+    ship_masked(1)
 
     def spread_grid(zz):
         @pl.loop(1, NX)
@@ -235,7 +239,8 @@
         out_ref[i] = jnp.concatenate(
             [got[zz, :, chunk * i:chunk * (i + 1)] for zz in range(NZ)], axis=1)
 
-    drain(parts.at[:, pl.ds(0, PLANE - 1)], rs_send)
+    for k in range(kdev):
+        drain(parts.at[k, pl.ds(0, PLANE - 1)], rs_send.at[k])
     drain(grid.at[0, pl.ds(0, NZ - 1)], grid_send)
     drain(grid.at[pl.ds(0, NX - 1)], gridx_send)
     drain(rows.at[0, pl.ds(0, NZ - 1)], rows_send)
@@ -274,7 +279,7 @@
             pltpu.VMEM((NZ, 2, kdev, 2 * chunk, 128), BF16),
             pltpu.VMEM((16, 8, 128), F32),
             pltpu.VMEM((NZ, 8, 128), F32),
-            dma, dma((kdev,)), dma, dma((NX, NZ)), dma, dma, dma((NY, NZ, kdev)), dma,
+            dma((kdev,)), dma((kdev,)), dma, dma((NX, NZ)), dma, dma, dma((NY, NZ, kdev)), dma,
             dma, dma, dma, dma, dma,
         ],
         compiler_params=pltpu.CompilerParams(

time: 80.6 us -> 80.1 us (level)
  no operation moved by 1% of the time
where the time goes in v6:
time: 80.1 us; the launch traced here: 79.3 us
  Pallas kernels  77.8 us (97%)
  local copies, waits for them, and re-layouts  1.52 us (2%)
    pallas_call x1, Pallas kernels, on_device(): pl.pallas_call(functools.partial(kernel, 1.0 / math.sqrt(total_k)), out_s...  77.8 us

profile of v6, /device:TPU:1, one launch (start us, length us, event | category | flops | bytes accessed | tf_op | source)
XLA Modules:
  0.0 79.3 jit_solution(6121915314607235177)
XLA Ops:
  0.0 77.8 %shard_map.37 = f32[4,8,512]{2,1,0:T(8,128)} custom-call(s32[2,128]{1,0:T(2,128)} %table_ref.1, s32[1,512]{1,0:T(1,128)} %bitcast.6, bf16[2,512,256]{2,1,0:T(8,128)(2,1)} %orbitals_ref.1), custom_call_target="tpu_custom_call" | custom-call | tf_op jit(solution)/shard_map/pallas_call | solution.py:266
  77.8 1.5 %copy.6 = f32[2,2,8,512]{3,1,0,2:T(2,128)} copy(f32[2,2,8,512]{3,2,1,0:T(8,128)} %bitcast.5) | data formatting | bytes 131072 | tf_op jit(solution)/shard_map/reshape | solution.py:288

commit v7 on v6

--- a/solution.py
+++ b/solution.py
@@ -183,8 +183,9 @@
                 if t < NZ // 2 - (ahead < 0):
                     pass_rows(zz, k, z + ahead)
                 spread_rows(zz, k)
-        for ship in ships[EARLY + t:EARLY + t + 1]:
-            ship_grid(*ship)
+            if k == 0:
+                for ship in ships[EARLY + t:EARLY + t + 1]:
+                    ship_grid(*ship)
         for zz in both_ways(t):
             drain(grid.at[x, zz], grid_recv.at[x, zz])
             spread_grid(zz)

time: 80.1 us -> 80.5 us (level)
  no operation moved by 1% of the time
where the time goes in v7:
time: 80.5 us; the launch traced here: 79.9 us
  Pallas kernels  78.4 us (97%)
  local copies, waits for them, and re-layouts  1.52 us (2%)
    pallas_call x1, Pallas kernels, on_device(): pl.pallas_call(functools.partial(kernel, 1.0 / math.sqrt(total_k)), out_s...  78.4 us

profile of v7, /device:TPU:1, one launch (start us, length us, event | category | flops | bytes accessed | tf_op | source)
XLA Modules:
  0.0 79.9 jit_solution(5307429427451778767)
XLA Ops:
  0.0 78.4 %shard_map.37 = f32[4,8,512]{2,1,0:T(8,128)} custom-call(s32[2,128]{1,0:T(2,128)} %table_ref.1, s32[1,512]{1,0:T(1,128)} %bitcast.6, bf16[2,512,256]{2,1,0:T(8,128)(2,1)} %orbitals_ref.1), custom_call_target="tpu_custom_call" | custom-call | tf_op jit(solution)/shard_map/pallas_call | solution.py:267
  78.4 1.5 %copy.6 = f32[2,2,8,512]{3,1,0,2:T(2,128)} copy(f32[2,2,8,512]{3,2,1,0:T(8,128)} %bitcast.5) | data formatting | bytes 131072 | tf_op jit(solution)/shard_map/reshape | solution.py:289
